TPU v7x, 256 devices: a whole 4x4x8 slice. The times are simulated.
256 devices in a mesh: leaf: 256 (over y, z, x, core).
Axes of the slice: x: 4, y: 4, z: 8, core: 2. Of those that a mesh axis runs over, the one named last changes fastest.
Arguments:
- measured: bfloat16 [16, 1048576], P(None, 'leaf'), may hold values from -6 to 6
- cluster_perm: int32 [256, 4096], P('leaf'), may hold values from 0 to 4095, each once within a row
- near_offsets: int32 [16384, 4], P('leaf'), may hold values from -2 to 2
- near_blocks: bfloat16 [16384, 64, 256], P('leaf'), may hold values from -0.375 to 0.375
- leaf_bases: bfloat16 [16384, 4096], P('leaf'), may hold values from -0.75 to 0.75
- local_transfer: bfloat16 [16128, 64, 128], P('leaf'), may hold values from -0.5 to 0.5
- coupling_pattern: int32 [32256, 2], P('leaf'), may hold values from 2 to 127, as said below
- local_coupling: bfloat16 [32256, 64, 128], P('leaf'), as said below
- root_transfer: bfloat16 [256, 4096], P('leaf'), may hold values from -0.5 to 0.5
- top_blocks: bfloat16 [256, 64, 128], replicated, as said below
Outputs:
- covariance_product: float32 [16, 1048576], P(None, 'leaf')
Inputs may be any that keep to these rules, and one draw needn't show every extreme that they name: `coupling_pattern`: row d * 126 + s - 2 belongs to slot s of subtree d; its entries are other slots of the same depth in that subtree. `local_coupling`: coupling blocks of the slots of each subtree in heap order. `top_blocks`: row 0 and the transfer half of row 1 are not used.
All inputs are finite; a program needn't handle non-finite values.
Results may differ from a plain program's by a relative error of at most 0.00065.
Values may be sent and summed in bfloat16 or wider, within the bound.
A program may use at most 128 MiB of HBM per device.

v0:
```python
import jax
import jax.numpy as jnp
from jax import lax
from jax.sharding import PartitionSpec as P

RANGE = 2


def padded_2(cells, sides, width):
    for axis, dim in sides:
        count = lax.axis_size(axis)
        ends = count - 1
        head = lax.slice_in_dim(cells, 0, width, axis=dim)
        tail = lax.slice_in_dim(cells, cells.shape[dim] - width, cells.shape[dim], axis=dim)
        cells = jnp.concatenate(
            [
                lax.ppermute(tail, axis, [(i, (i + 1) % count) for i in range(ends)]),
                cells,
                lax.ppermute(head, axis, [((i + 1) % count, i) for i in range(ends)]),
            ],
            axis=dim,
        )
    return cells


def climb_level(coeffs, pairing, groups):
    merged = coeffs.reshape(coeffs.shape[0], groups, 2, coeffs.shape[-1])
    return jnp.einsum(
        "rpci,picj->rpj",
        merged,
        pairing,
        precision=lax.Precision.HIGH,
        preferred_element_type=jnp.float32,
    )


def body(
    measured,
    cluster_perm,
    near_offsets,
    near_blocks,
    leaf_bases,
    local_transfer,
    coupling_pattern,
    local_coupling,
    root_transfer,
    top_blocks,
):
    highest = lax.Precision.HIGHEST
    doubled = lax.Precision.HIGH
    rhs_count = measured.shape[0]
    leaves = near_blocks.shape[0]
    leaf_size = near_blocks.shape[1]
    rank_size = local_transfer.shape[1]
    local_depth = leaves.bit_length() - 1
    ordering = cluster_perm[0]
    clustered = measured[:, ordering]
    padded = padded_2(clustered, (("leaf", 1),), RANGE * leaf_size)
    leaf_view = padded.reshape(rhs_count, leaves + 2 * RANGE, leaf_size)
    chosen = jnp.arange(leaves, dtype=jnp.int32)[:, None] + RANGE + near_offsets
    partners = leaf_view[:, chosen, :].reshape(rhs_count, leaves, -1)
    near_part = jnp.einsum(
        "lpq,rlq->rlp", near_blocks, partners, preferred_element_type=jnp.float32
    )
    leaf_basis = leaf_bases.reshape(leaves, leaf_size, rank_size)
    current = jnp.einsum(
        "rlp,lpk->rlk",
        clustered.reshape(rhs_count, leaves, leaf_size),
        leaf_basis,
        preferred_element_type=jnp.float32,
    )
    pairings = local_transfer.reshape(leaves - 1, rank_size, 2, rank_size)
    by_level = [current]
    for level_now in range(local_depth - 1, -1, -1):
        groups = 2**level_now
        current = climb_level(current, pairings[groups - 1 : 2 * groups - 1], groups)
        by_level.insert(0, current)
    root_coef = by_level[0][:, 0, :]
    root_map = root_transfer[0].astype(jnp.float32).reshape(rank_size, rank_size)
    root_up = jnp.einsum("ij,ri->rj", root_map, root_coef, precision=highest)
    top_table = top_blocks.astype(jnp.float32)
    devices = lax.axis_size("leaf")
    top_depth = devices.bit_length() - 1
    own_node = devices + lax.axis_index("leaf")
    siblings = []
    every_coef, every_up = (
        lax.all_gather(root_coef[None], "leaf", axis=0, tiled=True),
        lax.all_gather(root_up[None], "leaf", axis=0, tiled=True),
    )
    levels_top = {top_depth: every_coef}
    climbing = every_up
    for level_now in range(top_depth - 1, 0, -1):
        groups = 2**level_now
        parents = climbing[0::2] + climbing[1::2]
        levels_top[level_now] = parents
        if level_now > 1:
            climbing = jnp.einsum(
                "nij,nri->nrj",
                top_table[groups : 2 * groups, :, rank_size:],
                parents,
                precision=highest,
            )
    for bit_index in range(top_depth):
        level_now = top_depth - bit_index
        sibling_node = jnp.bitwise_xor(jnp.right_shift(own_node, bit_index), 1)
        siblings.append(
            lax.dynamic_index_in_dim(
                levels_top[level_now], sibling_node - 2**level_now, 0, keepdims=False
            )
        )
    field_now = jnp.zeros((rhs_count, rank_size), jnp.float32)
    for bit_index in range(top_depth - 1, -1, -1):
        node_now = jnp.right_shift(own_node, bit_index)
        pair_block = lax.dynamic_index_in_dim(
            top_table, jnp.right_shift(node_now, 1), 0, keepdims=False
        )[:, :rank_size]
        oriented = jnp.where(node_now % 2 == 0, pair_block, pair_block.T)
        coupled = jnp.einsum("ij,rj->ri", oriented, siblings[bit_index], precision=highest)
        if bit_index == 0:
            node_map = root_map
        else:
            node_map = lax.dynamic_index_in_dim(top_table, node_now, 0, keepdims=False)[
                :, rank_size:
            ]
        field_now = coupled + jnp.einsum("ij,rj->ri", node_map, field_now, precision=highest)
    stacked = jnp.concatenate(by_level[1:], axis=1)
    gathered = stacked[:, coupling_pattern - 2, :]
    couplings = local_coupling.reshape(2 * leaves - 2, rank_size, -1, rank_size)
    local_terms = jnp.einsum(
        "nicj,rncj->rni", couplings, gathered, precision=doubled, preferred_element_type=jnp.float32
    )
    current = field_now[:, None, :]
    for level_now in range(local_depth):
        groups = 2**level_now
        from_above = jnp.einsum(
            "picj,rpj->rpci",
            pairings[groups - 1 : 2 * groups - 1],
            current,
            precision=doubled,
            preferred_element_type=jnp.float32,
        ).reshape(rhs_count, 2 * groups, rank_size)
        current = local_terms[:, 2 * groups - 2 : 4 * groups - 2, :] + from_above
    far_part = jnp.einsum(
        "lpk,rlk->rlp", leaf_basis, current, precision=doubled, preferred_element_type=jnp.float32
    )
    combined = (near_part + far_part).reshape(rhs_count, -1)
    return jnp.zeros_like(combined).at[:, ordering].set(combined)


def solution(mesh):
    return jax.shard_map(
        body,
        mesh=mesh,
        in_specs=(
            P(None, "leaf"),
            P("leaf", None),
            P("leaf", None),
            P("leaf", None, None),
            P("leaf", None),
            P("leaf", None, None),
            P("leaf", None),
            P("leaf", None, None),
            P("leaf", None),
            P(),
        ),
        out_specs=P(None, "leaf"),
        check_vma=False,
    )
```

profile of v0, /device:TPU:1, one launch (start us, length us, event | category | flops | bytes accessed | tf_op | source)
XLA Modules:
  0.0 300.4 jit_solution(3947770605148678561)
XLA Ops:
  6.5 2.0 slice.171
  14.1 2.1 reshape.111
  16.2 3.2 %slice.172 = bf16[32,64,2,64]{3,2,1,0:T(2,128)(2,1)} reshape(bf16[32,64,128]{2,1,0:T(8,128)(2,1)} %slice.171) | data formatting | bytes 1048576 | tf_op jit(solution)/shard_map/slice | solution.py:76
  21.3 1.6 slice.178
  22.9 1.5 slice.180
  26.0 16.9 %gather_fusion = bf16[4096,16]{1,0:T(8,128)(2,1)} fusion(bf16[16,4096]{0,1:T(8,128)(2,1)} %copy.87, s32[4096]{0:T(1024)} %broadcast_clamp_fusion), kind=kCustom, calls=%fused_computation | custom fusion | bytes 278528 | tf_op jit(solution)/shard_map/gather | solution.py:57
  42.9 1.8 fusion.111
  50.7 4.5 %collective-permute-start = (bf16[16,128]{0,1:T(8,128)(2,1)}, bf16[16,128]{0,1:T(8,128)(2,1)}, u32[]{:S(2)}, u32[]{:S(2)}) collective-permute-start(bf16[16,128]{0,1:T(8,128)(2,1)} %get-tuple-element.20), channel_id=1, source_target_pairs={{0,1},{1,2},{2,3},{3,4},{4,5},{5,6},{6,7},{7,8},{8,9},{9,10},{10,1... | collective-permute-start | bytes 12296 | tf_op jit(solution)/shard_map/ppermute | solution.py:17
  55.2 2.7 collective-permute-start.1
  58.6 6.5 %convert_element_type.4 = f32[256,64,128]{2,1,0:T(8,128)} convert(bf16[256,64,128]{2,1,0:T(8,128)(2,1)} %param.19) | non-fusion elementwise | flops 2097152 | bytes 12582912 | tf_op jit(solution)/shard_map/convert_element_type | solution.py:81
  69.4 1.9 bitcast_dynamic-update-slice_fusion
  73.1 4.2 %copy.101 = bf16[126,64,128]{0,2,1:T(8,128)(2,1)} copy(bf16[126,64,128]{2,1,0:T(8,128)(2,1)} %param.17) | data formatting | bytes 4128768 | tf_op args[7]
  77.2 7.7 %copy.102 = bf16[126,64,2,64]{3,1,2,0:T(8,128)(2,1)} copy(bf16[126,64,2,64]{0,3,2,1:T(8,128)(2,1)} %bitcast.238) | data formatting | bytes 4128768 | tf_op jit(solution)/shard_map/reshape | solution.py:128
  85.0 3.3 %gather_fusion.2 = f32[252,16,64]{2,1,0:T(8,128)} fusion(f32[16,126,64]{2,0,1:T(8,128)} %bitcast_dynamic-update-slice_fusion, s32[1024]{0:T(1024)S(1)} %get-tuple-element.26), kind=kCustom, calls=%fused_computation.2 | custom fusion | bytes 2065392 | tf_op jit(solution)/shard_map/gather | solution.py:127
  88.3 6.0 %convolution_bitcast_fusion = f32[16,126,64]{2,0,1:T(8,128)} fusion(f32[16,126,2,64]{3,0,2,1:T(8,128)} %bitcast.239, bf16[126,64,2,64]{3,1,2,0:T(8,128)(2,1)} %copy.102), kind=kOutput, calls=%fused_computation.6 | convolution fusion | flops 99090432 | bytes 3612672 | tf_op jit(solution)/shard_map/nicj,rncj->rni/dot_general | solution.py:129
  95.8 1.5 dynamic-slice_bitcast_fusion
  97.3 1.6 copy.89
  108.8 1.8 gather_fusion.1
  110.6 2.8 copy.93
  113.4 2.7 reshape.109
  116.1 2.5 fusion.110
  118.6 39.0 %all-gather.7.cloned.1.call-done = f32[4096,64]{1,0:T(8,128)} async-done(((f32[16,64]{1,0:T(8,128)}), f32[4096,64]{1,0:T(8,128)}) %all-gather.7.cloned.1.call-update) | async-done | bytes 1048592 | tf_op jit(solution)/shard_map/all_gather | solution.py:88
  157.6 1.7 slice_add_fusion
  159.3 3.6 %fusion = f32[128,16,64]{2,1,0:T(8,128)S(1)} fusion(f32[128,16,64]{2,1,0:T(8,128)S(1)} %slice_add_fusion, bf16[256,64,128]{2,1,0:T(8,128)(2,1)} %param.19), kind=kOutput, calls=%fused_computation.4 | convolution fusion | flops 100663296 | bytes 3145728 | tf_op jit(solution)/shard_map/nij,nri->nrj/dot_general | solution.py:97
  163.0 2.3 fusion.6
  165.6 1.7 fusion.14
  174.5 90.0 %all-gather.5.cloned.1.call-done = f32[4096,1,64]{2,0,1:T(8,128)} async-done(((f32[16,1,64]{2,0,1:T(8,128)}), f32[4096,1,64]{2,0,1:T(8,128)}) %all-gather.5.cloned.1.call-update) | async-done | bytes 1048592 | tf_op jit(solution)/shard_map/all_gather | solution.py:87
  271.0 2.1 fusion.16
  273.1 1.7 fusion.10
  276.4 2.0 copy.119
  278.4 12.3 %scatter_custom_fusion = f32[16,4096]{0,1:T(8,128)} fusion(s32[4096]{0:T(1024)} %bitcast.266, f32[4096,16]{1,0:T(8,128)} %copy.119, f32[]{:T(128)} %constant.146.clone.1), kind=kCustom, calls=%fused_computation.25 | custom fusion | bytes 262656 | tf_op jit(solution)/shard_map/scatter | solution.py:147
  290.7 2.9 copy.120
  (180 shorter events, 48.2 us)
Async XLA Ops:
  6.5 109.6 %copy-start = (bf16[64,64,256]{2,1,0:T(8,128)(2,1)S(1)}, bf16[64,64,256]{2,1,0:T(8,128)(2,1)}, u32[]{:S(2)}) copy-start(bf16[64,64,256]{2,1,0:T(8,128)(2,1)} %param.13) | copy-start | bytes 6291460
  6.5 151.1 %all-gather.7.cloned.1.call-start = ((), (), s32[]{:S(2)}) async-start(), calls=%async_computation.1 | async-start | bytes 2105344 | tf_op jit(solution)/shard_map/all_gather | solution.py:88
  12.8 6.6 %slice-start = ((bf16[63,64,128]{2,1,0:T(8,128)(2,1)}), bf16[16,64,128]{2,1,0:T(8,128)(2,1)S(1)}, s32[]{:S(2)}) async-start(bf16[63,64,128]{2,1,0:T(8,128)(2,1)} %param.15), calls=%async_computation.2 | async-start | bytes 524288 | tf_op jit(solution)/shard_map/slice | solution.py:76
  14.1 10.3 %slice-start.2 = ((bf16[63,64,128]{2,1,0:T(8,128)(2,1)}), bf16[1,64,128]{2,1,0:T(8,128)(2,1)S(1)}, s32[]{:S(2)}) async-start(bf16[63,64,128]{2,1,0:T(8,128)(2,1)} %param.15), calls=%async_computation.4 | async-start | bytes 32768 | tf_op jit(solution)/shard_map/slice | solution.py:76
  49.2 215.3 %all-gather.5.cloned.1.call-start = ((), (), s32[]{:S(2)}) async-start(), calls=%async_computation | async-start | bytes 2105344 | tf_op jit(solution)/shard_map/all_gather | solution.py:87
  50.7 54.5 %collective-permute-start = (bf16[16,128]{0,1:T(8,128)(2,1)}, bf16[16,128]{0,1:T(8,128)(2,1)}, u32[]{:S(2)}, u32[]{:S(2)}) collective-permute-start(bf16[16,128]{0,1:T(8,128)(2,1)} %get-tuple-element.20), channel_id=1, source_target_pairs={{0,1},{1,2},{2,3},{3,4},{4,5},{5,6},{6,7},{7,8},{8,9},{9,10},{10,1... | collective-permute-start | bytes 12296 | tf_op jit(solution)/shard_map/ppermute | solution.py:17
  55.2 50.8 %collective-permute-start.1 = (bf16[16,128]{0,1:T(8,128)(2,1)}, bf16[16,128]{0,1:T(8,128)(2,1)}, u32[]{:S(2)}, u32[]{:S(2)}) collective-permute-start(bf16[16,128]{0,1:T(8,128)(2,1)} %get-tuple-element.21), channel_id=1, source_target_pairs={{1,0},{2,1},{3,2},{4,3},{5,4},{6,5},{7,6},{8,7},{9,8},{10,9},{11,1... | collective-permute-start | bytes 12296 | tf_op jit(solution)/shard_map/ppermute | solution.py:19
  97.3 8.7 %copy-start.14 = (f32[64,128]{1,0:T(8,128)}, f32[64,128]{1,0:T(8,128)S(1)}, u32[]{:S(2)}) copy-start(f32[64,128]{1,0:T(8,128)S(1)} %get-tuple-element.12) | copy-start | bytes 98308
  97.3 8.7 %copy-start.15 = (f32[64,128]{1,0:T(8,128)}, f32[64,128]{1,0:T(8,128)S(1)}, u32[]{:S(2)}) copy-start(f32[64,128]{1,0:T(8,128)S(1)} %get-tuple-element.11) | copy-start | bytes 98308
  97.3 8.7 %copy-start.17 = (f32[64,128]{1,0:T(8,128)}, f32[64,128]{1,0:T(8,128)S(1)}, u32[]{:S(2)}) copy-start(f32[64,128]{1,0:T(8,128)S(1)} %get-tuple-element.10) | copy-start | bytes 98308
  97.3 8.7 %copy-start.19 = (f32[64,128]{1,0:T(8,128)}, f32[64,128]{1,0:T(8,128)S(1)}, u32[]{:S(2)}) copy-start(f32[64,128]{1,0:T(8,128)S(1)} %get-tuple-element.9) | copy-start | bytes 98308
  97.3 13.3 %copy-start.21 = (f32[64,128]{1,0:T(8,128)}, f32[64,128]{1,0:T(8,128)S(1)}, u32[]{:S(2)}) copy-start(f32[64,128]{1,0:T(8,128)S(1)} %get-tuple-element.8) | copy-start | bytes 98308
  97.3 13.3 %copy-start.24 = (f32[64,128]{1,0:T(8,128)}, f32[64,128]{1,0:T(8,128)S(1)}, u32[]{:S(2)}) copy-start(f32[64,128]{1,0:T(8,128)S(1)} %get-tuple-element.7) | copy-start | bytes 98308
  97.3 13.2 %copy-start.26 = (f32[64,128]{1,0:T(8,128)}, f32[64,128]{1,0:T(8,128)S(1)}, u32[]{:S(2)}) copy-start(f32[64,128]{1,0:T(8,128)S(1)} %get-tuple-element.6) | copy-start | bytes 98308
  165.4 6.6 %copy-start.42 = (bf16[64,128]{1,0:T(8,128)(2,1)S(1)}, bf16[64,128]{1,0:T(8,128)(2,1)}, u32[]{:S(2)}) copy-start(bf16[64,128]{1,0:T(8,128)(2,1)} %get-tuple-element.16) | copy-start | bytes 49156
  165.4 6.8 %copy-start.22 = (f32[64,128]{1,0:T(8,128)S(1)}, f32[64,128]{1,0:T(8,128)}, u32[]{:S(2)}) copy-start(f32[64,128]{1,0:T(8,128)} %copy-done.21) | copy-start | bytes 98308
  165.4 6.9 %copy-start.33 = (f32[64,64]{0,1:T(8,128)S(1)}, f32[64,64]{0,1:T(8,128)}, u32[]{:S(2)}) copy-start(f32[64,64]{0,1:T(8,128)} %copy.108) | copy-start | bytes 49156
  165.4 7.0 %copy-start.41 = (bf16[64,128]{1,0:T(8,128)(2,1)S(1)}, bf16[64,128]{1,0:T(8,128)(2,1)}, u32[]{:S(2)}) copy-start(bf16[64,128]{1,0:T(8,128)(2,1)} %get-tuple-element.15) | copy-start | bytes 49156
  165.4 7.2 %copy-start.20 = (f32[64,128]{1,0:T(8,128)S(1)}, f32[64,128]{1,0:T(8,128)}, u32[]{:S(2)}) copy-start(f32[64,128]{1,0:T(8,128)} %copy-done.19) | copy-start | bytes 98308
  165.4 7.2 %copy-start.34 = (f32[64,64]{0,1:T(8,128)S(1)}, f32[64,64]{0,1:T(8,128)}, u32[]{:S(2)}) copy-start(f32[64,64]{0,1:T(8,128)} %copy.107) | copy-start | bytes 49156
  165.4 7.4 %copy-start.40 = (bf16[64,128]{1,0:T(8,128)(2,1)S(1)}, bf16[64,128]{1,0:T(8,128)(2,1)}, u32[]{:S(2)}) copy-start(bf16[64,128]{1,0:T(8,128)(2,1)} %get-tuple-element.14) | copy-start | bytes 49156
  165.5 7.6 %copy-start.18 = (f32[64,128]{1,0:T(8,128)S(1)}, f32[64,128]{1,0:T(8,128)}, u32[]{:S(2)}) copy-start(f32[64,128]{1,0:T(8,128)} %copy-done.17) | copy-start | bytes 98308
  165.5 7.6 %copy-start.35 = (f32[64,64]{0,1:T(8,128)S(1)}, f32[64,64]{0,1:T(8,128)}, u32[]{:S(2)}) copy-start(f32[64,64]{0,1:T(8,128)} %copy.106) | copy-start | bytes 49156
  165.5 7.8 %copy-start.39 = (bf16[64,128]{1,0:T(8,128)(2,1)S(1)}, bf16[64,128]{1,0:T(8,128)(2,1)}, u32[]{:S(2)}) copy-start(bf16[64,128]{1,0:T(8,128)(2,1)} %get-tuple-element.19) | copy-start | bytes 49156
  165.5 8.0 %copy-start.16 = (f32[64,128]{1,0:T(8,128)S(1)}, f32[64,128]{1,0:T(8,128)}, u32[]{:S(2)}) copy-start(f32[64,128]{1,0:T(8,128)} %copy-done.15) | copy-start | bytes 98308
  165.5 8.0 %copy-start.36 = (f32[64,64]{0,1:T(8,128)S(1)}, f32[64,64]{0,1:T(8,128)}, u32[]{:S(2)}) copy-start(f32[64,64]{0,1:T(8,128)} %copy.105) | copy-start | bytes 49156
  165.5 8.2 %copy-start.38 = (bf16[64,128]{1,0:T(8,128)(2,1)S(1)}, bf16[64,128]{1,0:T(8,128)(2,1)}, u32[]{:S(2)}) copy-start(bf16[64,128]{1,0:T(8,128)(2,1)} %get-tuple-element.13) | copy-start | bytes 49156
  165.6 103.0 %copy-start.10 = (bf16[4,64,2,64]{3,2,1,0:T(2,128)(2,1)S(1)}, bf16[4,64,2,64]{3,2,1,0:T(2,128)(2,1)}, u32[]{:S(2)}) copy-start(bf16[4,64,2,64]{3,2,1,0:T(2,128)(2,1)} %slice.178) | copy-start | bytes 196612
  165.6 104.1 %copy-start.7 = (bf16[8,64,2,64]{3,2,1,0:T(2,128)(2,1)S(1)}, bf16[8,64,2,64]{3,2,1,0:T(2,128)(2,1)}, u32[]{:S(2)}) copy-start(bf16[8,64,2,64]{3,2,1,0:T(2,128)(2,1)} %slice.176) | copy-start | bytes 393220
  264.5 8.5 %copy-start.2 = (bf16[32,64,2,64]{3,2,1,0:T(2,128)(2,1)S(1)}, bf16[32,64,2,64]{3,2,1,0:T(2,128)(2,1)}, u32[]{:S(2)}) copy-start(bf16[32,64,2,64]{3,2,1,0:T(2,128)(2,1)} %slice.172) | copy-start | bytes 1572868
  264.5 8.5 %copy-start.5 = (f32[16,126,64]{2,0,1:T(8,128)S(1)}, f32[16,126,64]{2,0,1:T(8,128)}, u32[]{:S(2)}) copy-start(f32[16,126,64]{2,0,1:T(8,128)} %convolution_bitcast_fusion) | copy-start | bytes 1548292
  265.6 9.2 %copy-start.8 = (f32[64,16,64]{2,1,0:T(8,128)S(1)}, f32[64,16,64]{2,1,0:T(8,128)}, u32[]{:S(2)}) copy-start(f32[64,16,64]{2,1,0:T(8,128)} %fusion.110) | copy-start | bytes 786436
  (21 other events, 78.8 us)
Sparse Core Ops, SparseCore 0:
  49.4 108.2 all-gather.6
  161.3 103.1 all-gather.4
where the time goes:
time: 303 us; the launch traced here: 300 us
  waiting for transfers between devices  129 us (43%)
  local copies, waits for them, and re-layouts  98 us (32%)
  matrix products  39.5 us (13%)
  between operations  14.1 us (5%)
  other arithmetic  12.5 us (4%)
  starting transfers between devices  7.24 us (2%)
    all_gather x1, waiting for transfers between devices, body(): lax.all_gather(root_coef[None], 'leaf', axis=0, tiled=True)  90 us
    all_gather x1, waiting for transfers between devices, body(): lax.all_gather(root_up[None], 'leaf', axis=0, tiled=True)  39 us
    gather x2, local copies, waits for them, and re-layouts, body(): clustered = measured[:, ordering]  18.5 us
    scatter x2, local copies, waits for them, and re-layouts, body(): return jnp.zeros_like(combined).at[:, ordering].set(combined)  15.2 us
    slice x14, local copies, waits for them, and re-layouts, body(): current = climb_level(current, pairings[groups - 1:2 * groups - 1], groups)  13 us
    unnamed x98, local copies, waits for them, and re-layouts  11.3 us
    dot_general x6, matrix products, body(): jnp.einsum('nij,nri->nrj', top_table[groups:2 * groups, :, rank_size:], p...  11.2 us
    dot_general x6, matrix products, body(): jnp.einsum('picj,rpj->rpci', pairings[groups - 1:2 * groups - 1], current...  8.24 us
  transfers between devices with their start and end apart: 4, of which 2 were waited for; matrix products, arithmetic and copies ran while one was open for 26% of the time, Pallas kernels for 0%

commit v1 on v0

v1 whole, which is shorter than its diff:
```python
import jax
import jax.numpy as jnp
from jax import lax
from jax.experimental import pallas as pl
from jax.experimental.pallas import tpu as pltpu
from jax.sharding import PartitionSpec as P

F32 = jnp.float32
BF16 = jnp.bfloat16
MESH = pl.DeviceIdType.MESH
NRHS = 16
RANK = 64
LEAVES = 64
POINTS = 4096
SPAN = 256
CHUNKS = POINTS // SPAN
COARSE = POINTS // SPAN

TOP_ROWS = [(7, 0), (7, 1), (7, 2), (7, 3), (6, 0), (6, 1), (5, 0)]
TOP_ROWS += [(4, 0), (4, 1), (4, 2), (4, 3), (3, 0), (3, 1), (2, 0), (1, 0), (0, 0)]
TOP_SLOT = {row: slot for slot, row in enumerate(TOP_ROWS)}


def nn(a, b):
    return lax.dot_general(a, b, (((1,), (0,)), ((), ())), preferred_element_type=F32)


def nt(a, b):
    return lax.dot_general(a, b, (((1,), (1,)), ((), ())), preferred_element_type=F32)


def flipped(index, mask):
    out = index
    for bit in range(8):
        if (mask >> bit) & 1:
            step = 1 << bit
            out = out + step * (1 - 2 * lax.rem(lax.div(index, step), 2))
    return out


def split(x):
    high = x.astype(BF16)
    return high, (x - high.astype(F32)).astype(BF16)


def stacked(x):
    return jnp.concatenate(split(x), axis=0)[:, :RANK]


def folded(x):
    return x[0:NRHS] + x[NRHS : 2 * NRHS]


def swapped(x):
    return pltpu.roll(x, RANK, axis=1)


def kernel(
    offsets,
    pattern,
    measured_hbm,
    perm_hbm,
    near_hbm,
    bases_hbm,
    transfer_hbm,
    coupling_hbm,
    root_hbm,
    top_hbm,
    out,
    measured,
    perm,
    near_blocks,
    bases,
    transfer,
    coupling,
    root_row,
    tops,
    tops_swapped,
    root_wide,
    basis_wide,
    basis,
    onehot,
    points,
    coef,
    local_terms,
    near_part,
    fields,
    combined,
    edges,
    halo,
    first,
    second,
    third,
    in_sem,
    top_sem,
    halo_send,
    halo_recv,
    first_send,
    first_recv,
    second_send,
    second_recv,
    third_send,
    third_recv,
):
    me = lax.axis_index("leaf")
    right = lax.rem(me + 1, 256)
    left = lax.rem(me + 255, 256)
    low = lax.broadcasted_iota(jnp.int32, (NRHS, 128), 1) < RANK

    loads = [
        pltpu.make_async_copy(source, target, in_sem.at[i])
        for i, (source, target) in enumerate(
            [
                (perm_hbm, perm),
                (measured_hbm, measured),
                (bases_hbm, bases),
                (root_hbm, root_row),
                (transfer_hbm, transfer),
                (coupling_hbm, coupling),
                (near_hbm, near_blocks),
            ]
        )
    ]
    for load in loads[:5]:
        load.start()
    top_loads = []
    for slot, (level, relative) in enumerate(TOP_ROWS):
        node = (1 << level) + flipped(lax.div(me, 1 << (8 - level)), relative)
        top_loads.append(pltpu.make_async_copy(top_hbm.at[node], tops.at[slot], top_sem.at[slot]))
        top_loads[-1].start()
    for load in loads[5:]:
        load.start()

    barrier = pltpu.get_barrier_semaphore()
    peers = [flipped(me, k) for k in range(1, 8)]
    peers += [flipped(me, 8 * k) for k in range(1, 8)]
    peers += [flipped(me, 64 * k) for k in range(1, 4)]
    peers += [left, right]
    for peer in peers:
        pl.semaphore_signal(barrier, inc=1, device_id=(peer,), device_id_type=MESH)

    loads[0].wait()
    loads[1].wait()
    spread = jnp.concatenate(
        [measured[:, h * SPAN : (h + 1) * SPAN] for h in range(COARSE)], axis=0
    )
    rows = lax.broadcasted_iota(jnp.int32, (SPAN, SPAN), 0)
    for c in range(CHUNKS):
        at = slice(c * SPAN, (c + 1) * SPAN)
        order = perm[0:1, at]
        hot = jnp.where(rows == lax.rem(order, SPAN), 1.0, 0.0).astype(BF16)
        onehot[:, at] = hot
        picked = nn(spread, hot)
        coarse = jnp.broadcast_to(lax.div(order, SPAN), (NRHS, SPAN))
        chosen = picked[0:NRHS]
        for h in range(1, COARSE):
            chosen = jnp.where(coarse == h, picked[h * NRHS : (h + 1) * NRHS], chosen)
        for pair in range(2):
            both = chosen[:, pair * 128 : (pair + 1) * 128]
            turned = swapped(both)
            leaf = 4 * c + 2 * pair
            points[leaf + 2] = jnp.where(low, both, turned).astype(BF16)
            points[leaf + 3] = jnp.where(low, turned, both).astype(BF16)
            if leaf == 0:
                edges[0] = both.astype(BF16)
            if leaf == LEAVES - 2:
                edges[1] = both.astype(BF16)

    pl.semaphore_wait(barrier, len(peers))
    halo_copies = [
        pltpu.make_async_remote_copy(
            src_ref=edges.at[side],
            dst_ref=halo.at[side],
            send_sem=halo_send.at[side],
            recv_sem=halo_recv.at[side],
            device_id=(target,),
            device_id_type=MESH,
        )
        for side, target in ((0, left), (1, right))
    ]
    for copy in halo_copies:
        copy.start()

    loads[2].wait()
    low_leaves = lax.broadcasted_iota(jnp.int32, (LEAVES, 128), 1) < RANK
    for pair in range(32):
        both = bases[:, pair * 128 : (pair + 1) * 128].astype(F32)
        turned = swapped(both)
        basis_wide[pl.ds(2 * pair, LEAVES, stride=RANK), :] = jnp.where(low_leaves, both, turned)
        basis_wide[pl.ds(2 * pair + 1, LEAVES, stride=RANK), :] = jnp.where(low_leaves, turned, both)
    basis[...] = basis_wide[...].astype(BF16)

    loads[3].wait()
    low_row = lax.broadcasted_iota(jnp.int32, (1, 128), 1) < RANK
    for pair in range(32):
        both = root_row[0:1, pair * 128 : (pair + 1) * 128].astype(F32)
        turned = swapped(both)
        root_wide[2 * pair : 2 * pair + 1, :] = jnp.where(low_row, both, turned)
        root_wide[2 * pair + 1 : 2 * pair + 2, :] = jnp.where(low_row, turned, both)
    root_map = root_wide[...].astype(BF16)

    quarter = lax.broadcasted_iota(jnp.int32, (NRHS, 256), 1) // RANK
    for four in range(LEAVES // 4):
        lanes = [points[2 + 4 * four + k].astype(F32) for k in range(4)]
        wide = [
            jnp.concatenate([lanes[k], lanes[k]], axis=1) for k in range(4)
        ]
        block = jnp.concatenate(
            [jnp.where(quarter == k, wide[k], 0.0) for k in range(4)], axis=0
        ).astype(BF16)
        result = nn(block, basis[four * 256 : (four + 1) * 256, :])
        for k in range(4):
            coef[64 + 4 * four + k] = jnp.concatenate(
                split(result[k * NRHS : (k + 1) * NRHS]), axis=0
            )

    loads[4].wait()

    def climb(parent):
        children = coef[pl.ds(2 * parent, 2)].reshape(64, 128)[:, :RANK]
        result = nn(children, transfer[parent - 1])
        mixed = jnp.where(low, folded(result[0:32]), folded(result[32:64]))
        return mixed + swapped(mixed)

    for level in range(5, 0, -1):
        groups = 1 << level
        for parent in range(groups, 2 * groups):
            coef[parent] = jnp.concatenate(split(climb(parent)), axis=0)
    root_coef = climb(1)
    root_up = folded(nn(stacked(root_coef), root_map))
    first[0] = jnp.where(low, root_up, root_coef)

    def exchange(buffer, count, shift, send_sem, recv_sem):
        copies = [
            pltpu.make_async_remote_copy(
                src_ref=buffer.at[0],
                dst_ref=buffer.at[k],
                send_sem=send_sem.at[k],
                recv_sem=recv_sem.at[k],
                device_id=(flipped(me, k << shift),),
                device_id_type=MESH,
            )
            for k in range(1, count)
        ]
        for copy in copies:
            copy.start()
        return copies

    first_copies = exchange(first, 8, 0, first_send, first_recv)

    for load in top_loads:
        load.wait()
    for slot in range(len(TOP_ROWS)):
        tops_swapped[slot] = swapped(tops[slot].astype(F32)).astype(BF16)

    loads[5].wait()

    def couple(pair):
        sides = []
        for k in range(2):
            n = 2 * pair + k
            sides.append(
                jnp.concatenate(
                    [coef[pattern[0, n]][:, :RANK], coef[pattern[1, n]][:, RANK:]], axis=1
                )
            )
        blocks = coupling[pl.ds(2 * pair, 2)].reshape(128, 128)
        result = nt(jnp.concatenate(sides, axis=0), blocks)
        local_terms[pair + 1] = jnp.where(low, folded(result[0:32]), folded(result[32:64]))

    def near(pair):
        sides = []
        for k in range(2):
            leaf = 2 * pair + k
            at = [points[leaf + 2 + offsets[j, leaf]] for j in range(4)]
            sides.append(
                jnp.concatenate(
                    [at[0][:, :RANK], at[1][:, RANK:], at[2][:, :RANK], at[3][:, RANK:]], axis=1
                )
            )
        blocks = near_blocks[pl.ds(2 * pair, 2)].reshape(128, 256)
        result = nt(jnp.concatenate(sides, axis=0), blocks)
        near_part[pair] = jnp.where(low, result[0:NRHS], result[NRHS : 2 * NRHS])

    @pl.loop(0, 9)
    def _(step):
        for k in range(7):
            couple(7 * step + k)

    def lift(values, level):
        return [
            folded(nn(stacked(value), tops_swapped[TOP_SLOT[level, k]]))
            for k, value in enumerate(values)
        ]

    def added(values):
        return [values[2 * k] + values[2 * k + 1] for k in range(len(values) // 2)]

    def coupled(sibling, level):
        block = tops[TOP_SLOT[level - 1, 0]]
        parts = stacked(sibling)
        to_left = folded(nt(parts, block[:, :RANK]))
        to_right = folded(nn(parts, block))[:, :RANK]
        odd = lax.rem(lax.div(me, 1 << (8 - level)), 2)
        return jnp.where(odd == 1, to_right, to_left)

    terms = {}
    for copy in first_copies:
        copy.wait()
    at_7 = added([first[k] for k in range(8)])
    at_6 = added(lift(at_7, 7))
    at_5 = added(lift(at_6, 6))[0]
    second[0] = jnp.where(low, lift([at_5], 5)[0], swapped(at_5))
    second_copies = exchange(second, 8, 3, second_send, second_recv)
    terms[8] = coupled(swapped(first[1]), 8)
    terms[7] = coupled(at_7[1], 7)
    terms[6] = coupled(at_6[1], 6)

    for copy in halo_copies:
        copy.wait()
    for side, leaf, end in ((1, 0, 0), (0, 66, 255)):
        both = jnp.where(me == end, 0.0, halo[side].astype(F32))
        turned = swapped(both)
        points[leaf] = jnp.where(low, both, turned).astype(BF16)
        points[leaf + 1] = jnp.where(low, turned, both).astype(BF16)
    loads[6].wait()

    @pl.loop(0, 4)
    def _(step):
        for k in range(8):
            near(8 * step + k)

    for copy in second_copies:
        copy.wait()
    at_4 = added([second[k] for k in range(8)])
    at_3 = added(lift(at_4, 4))
    at_2 = added(lift(at_3, 3))[0]
    third[0] = jnp.where(low, lift([at_2], 2)[0], swapped(at_2))
    third_copies = exchange(third, 4, 6, third_send, third_recv)
    terms[5] = coupled(swapped(second[1]), 5)
    terms[4] = coupled(at_4[1], 4)
    terms[3] = coupled(at_3[1], 3)

    for copy in third_copies:
        copy.wait()
    at_1 = added([third[k] for k in range(4)])
    terms[2] = coupled(swapped(third[1]), 2)
    terms[1] = coupled(at_1[1], 1)
    field = terms[1]
    for level in range(2, 8):
        block = tops_swapped[TOP_SLOT[level, 0]][:, :RANK]
        field = terms[level] + folded(nt(stacked(field), block))
    field = terms[8] + folded(nt(stacked(field), root_map[:, :RANK]))

    def descend(parent, here, there):
        lhs = jnp.concatenate(
            [jnp.where(low, part, 0.0) for part in here]
            + [jnp.where(low, 0.0, part) for part in there],
            axis=0,
        ).astype(BF16)
        block = transfer[parent - 1]
        result = nt(lhs, jnp.concatenate([block, block], axis=0))
        fields[parent] = local_terms[parent] + jnp.where(
            low, folded(result[0:32]), folded(result[32:64])
        )

    def parts_of(x):
        high = x.astype(BF16).astype(F32)
        return high, x - high

    root_parts = parts_of(jnp.concatenate([field, field], axis=1))
    descend(1, root_parts, root_parts)
    for level in range(5):
        for q in range(1 << level, 2 << level):
            pair = fields[q]
            straight = parts_of(pair)
            crossed = parts_of(swapped(pair))
            descend(2 * q, straight, crossed)
            descend(2 * q + 1, crossed, straight)

    for m in range(32):
        pair = fields[32 + m]
        lhs = jnp.concatenate(split(pair) + split(swapped(pair)), axis=0)[:, :RANK]
        result = nt(lhs, basis[m * 128 : (m + 1) * 128, :RANK])
        whole = near_part[m] + jnp.where(low, folded(result[0:32]), folded(result[32:64]))
        combined[:, m * 128 : (m + 1) * 128] = jnp.concatenate(parts_of(whole), axis=0)

    total = jnp.zeros((COARSE * 32, SPAN), F32)
    for c in range(CHUNKS):
        at = slice(c * SPAN, (c + 1) * SPAN)
        coarse = jnp.broadcast_to(lax.div(perm[0:1, at], SPAN), (32, SPAN))
        values = combined[:, at]
        lhs = jnp.concatenate(
            [jnp.where(coarse == h, values, 0.0) for h in range(COARSE)], axis=0
        ).astype(BF16)
        total = total + nt(lhs, onehot[:, at])
    for h in range(COARSE):
        out[:, h * SPAN : (h + 1) * SPAN] = folded(total[h * 32 : (h + 1) * 32])


def body(
    measured,
    cluster_perm,
    near_offsets,
    near_blocks,
    leaf_bases,
    local_transfer,
    coupling_pattern,
    local_coupling,
    root_transfer,
    top_blocks,
):
    smem = pl.BlockSpec(memory_space=pltpu.SMEM)
    hbm = pl.BlockSpec(memory_space=pl.ANY)
    dma = pltpu.SemaphoreType.DMA
    return pl.pallas_call(
        kernel,
        out_shape=jax.ShapeDtypeStruct((NRHS, POINTS), F32),
        in_specs=[smem, smem] + [hbm] * 8,
        out_specs=pl.BlockSpec(memory_space=pltpu.VMEM),
        scratch_shapes=[
            pltpu.VMEM((NRHS, POINTS), BF16),
            pltpu.VMEM((1, POINTS), jnp.int32),
            pltpu.VMEM((64, 64, 256), BF16),
            pltpu.VMEM((64, 4096), BF16),
            pltpu.VMEM((63, 64, 128), BF16),
            pltpu.VMEM((126, 64, 128), BF16),
            pltpu.VMEM((1, 4096), BF16),
            pltpu.VMEM((16, 64, 128), BF16),
            pltpu.VMEM((16, 64, 128), BF16),
            pltpu.VMEM((64, 128), F32),
            pltpu.VMEM((4096, 128), F32),
            pltpu.VMEM((4096, 128), BF16),
            pltpu.VMEM((SPAN, POINTS), BF16),
            pltpu.VMEM((68, NRHS, 128), BF16),
            pltpu.VMEM((128, 2 * NRHS, 128), BF16),
            pltpu.VMEM((64, NRHS, 128), F32),
            pltpu.VMEM((32, NRHS, 128), F32),
            pltpu.VMEM((64, NRHS, 128), F32),
            pltpu.VMEM((2 * NRHS, POINTS), F32),
            pltpu.VMEM((2, NRHS, 128), BF16),
            pltpu.VMEM((2, NRHS, 128), BF16),
            pltpu.VMEM((8, NRHS, 128), F32),
            pltpu.VMEM((8, NRHS, 128), F32),
            pltpu.VMEM((4, NRHS, 128), F32),
            dma((7,)),
            dma((16,)),
            dma((2,)),
            dma((2,)),
            dma((8,)),
            dma((8,)),
            dma((8,)),
            dma((8,)),
            dma((4,)),
            dma((4,)),
        ],
        compiler_params=pltpu.CompilerParams(
            collective_id=0, has_side_effects=True, vmem_limit_bytes=40 * 1024 * 1024
        ),
    )(
        near_offsets.T,
        coupling_pattern.T,
        measured,
        cluster_perm,
        near_blocks,
        leaf_bases,
        local_transfer,
        local_coupling,
        root_transfer,
        top_blocks,
    )


def solution(mesh):
    return jax.shard_map(
        body,
        mesh=mesh,
        in_specs=(
            P(None, "leaf"),
            P("leaf", None),
            P("leaf", None),
            P("leaf", None, None),
            P("leaf", None),
            P("leaf", None, None),
            P("leaf", None),
            P("leaf", None, None),
            P("leaf", None),
            P(),
        ),
        out_specs=P(None, "leaf"),
        check_vma=False,
    )
```

time: 303 us -> 45.7 us (0.15)
  waiting for transfers between devices: 129 us -> 0 us
  local copies, waits for them, and re-layouts: 98 us -> 12 us
  matrix products: 39.5 us -> 0 us
  Pallas kernels: 0 us -> 33.2 us
  between operations: 14.1 us -> 0.02 us
  other arithmetic: 12.5 us -> 0 us
  starting transfers between devices: 7.24 us -> 0 us
    all_gather x2 -> x0, waiting for transfers between devices: 129 us -> none  [the longest x1 90 us: body(): lax.all_gather(root_coef[None], 'leaf', axis=0, tiled=True)]
    dot_general x39 -> x0, matrix products: 39.5 us -> none  [the longest x6 11.2 us: body(): jnp.einsum('nij,nri->nrj', top_table[groups:2 * groups, :, rank_size:], p...]
    pallas_call x0 -> x1, Pallas kernels: none -> 33.2 us  [body(): pl.pallas_call(kernel, out_shape=jax.ShapeDtypeStruct((NRHS, POINTS), F32...]
    gather x5 -> x0, local copies, waits for them, and re-layouts: 26.3 us -> none  [the longest x2 18.5 us: body(): clustered = measured[:, ordering]]
    slice x24 -> x0, local copies, waits for them, and re-layouts: 20.7 us -> none  [the longest x14 13 us: body(): current = climb_level(current, pairings[groups - 1:2 * groups - 1], groups)]
    reshape x8 -> x0, local copies, waits for them, and re-layouts: 16.7 us -> none  [the longest x1 7.74 us: body(): couplings = local_coupling.reshape(2 * leaves - 2, rank_size, -1, rank_size)]
    scatter x2 -> x0, local copies, waits for them, and re-layouts: 15.2 us -> none  [body(): return jnp.zeros_like(combined).at[:, ordering].set(combined)]
    ppermute x2 -> x0, starting transfers between devices: 7.2 us -> none  [the longest x1 4.5 us: padded_2(): lax.ppermute(tail, axis, [(i, (i + 1) % count) for i in range(ends)])]
  transfers between devices with their start and end apart: 4 -> 0, of which waited for: 2 -> 0; matrix products, arithmetic and copies ran while one was open for 26% -> 0% of each run, Pallas kernels for 0% -> 0%
where the time goes in v1:
time: 45.7 us; the launch traced here: 45.3 us
  Pallas kernels  33.2 us (73%)
  local copies, waits for them, and re-layouts  12 us (26%)
    pallas_call x1, Pallas kernels, body(): pl.pallas_call(kernel, out_shape=jax.ShapeDtypeStruct((NRHS, POINTS), F32...  33.2 us
    unnamed x21, local copies, waits for them, and re-layouts  12 us

profile of v1, /device:TPU:1, one launch (start us, length us, event | category | flops | bytes accessed | tf_op | source)
XLA Modules:
  0.0 45.3 jit_solution(12059394987091693368)
XLA Ops:
  0.0 0.0 copy-start
  0.0 2.2 %copy-done = bf16[256,64,128]{2,1,0:T(8,128)(2,1)S(1)} copy-done((bf16[256,64,128]{2,1,0:T(8,128)(2,1)S(1)}, bf16[256,64,128]{2,1,0:T(8,128)(2,1)}, u32[]{:S(2)}) %copy-start) | copy-done | bytes 4194328
  2.2 0.0 copy-start.1
  2.2 1.6 %copy-done.1 = bf16[64,64,256]{2,1,0:T(8,128)(2,1)S(1)} copy-done((bf16[64,64,256]{2,1,0:T(8,128)(2,1)S(1)}, bf16[64,64,256]{2,1,0:T(8,128)(2,1)}, u32[]{:S(2)}) %copy-start.1) | copy-done | bytes 2097176
  3.8 0.0 copy-start.2
  3.8 1.6 %copy-done.2 = bf16[126,64,128]{2,1,0:T(8,128)(2,1)S(1)} copy-done((bf16[126,64,128]{2,1,0:T(8,128)(2,1)S(1)}, bf16[126,64,128]{2,1,0:T(8,128)(2,1)}, u32[]{:S(2)}) %copy-start.2) | copy-done | bytes 2064408
  5.4 0.0 copy-start.3
  5.4 1.2 %copy-done.3 = bf16[63,64,128]{2,1,0:T(8,128)(2,1)S(1)} copy-done((bf16[63,64,128]{2,1,0:T(8,128)(2,1)S(1)}, bf16[63,64,128]{2,1,0:T(8,128)(2,1)}, u32[]{:S(2)}) %copy-start.3) | copy-done | bytes 1032216
  6.6 0.0 copy-start.4
  6.6 1.0 %copy-done.4 = bf16[64,4096]{1,0:T(8,128)(2,1)S(1)} copy-done((bf16[64,4096]{1,0:T(8,128)(2,1)S(1)}, bf16[64,4096]{1,0:T(8,128)(2,1)}, u32[]{:S(2)}) %copy-start.4) | copy-done | bytes 524312
  7.6 0.0 copy-start.5
  7.6 0.9 %copy-done.5 = bf16[16,4096]{1,0:T(8,128)(2,1)S(1)} copy-done((bf16[16,4096]{1,0:T(8,128)(2,1)S(1)}, bf16[16,4096]{1,0:T(8,128)(2,1)}, u32[]{:S(2)}) %copy-start.5) | copy-done | bytes 131096
  8.5 0.0 copy-start.6
  8.5 0.7 %copy-done.6 = s32[1,4096]{1,0:T(1,128)S(1)} copy-done((s32[1,4096]{1,0:T(1,128)S(1)}, s32[1,4096]{1,0:T(1,128)}, u32[]{:S(2)}) %copy-start.6) | copy-done | bytes 16408
  9.2 0.0 copy-start.7
  9.2 0.7 %copy-done.7 = bf16[1,4096]{1,0:T(2,128)(2,1)S(1)} copy-done((bf16[1,4096]{1,0:T(2,128)(2,1)S(1)}, bf16[1,4096]{1,0:T(2,128)(2,1)}, u32[]{:S(2)}) %copy-start.7) | copy-done | bytes 8216
  10.0 0.0 copy-start.8
  10.0 0.7 %copy-done.8 = s32[64,4]{0,1:T(4,128)S(1)} copy-done((s32[64,4]{0,1:T(4,128)S(1)}, s32[64,4]{0,1:T(4,128)}, u32[]{:S(2)}) %copy-start.8) | copy-done | bytes 1048
  10.6 0.0 copy-start.9
  10.6 0.7 %copy-done.9 = s32[126,2]{0,1:T(2,128)S(1)} copy-done((s32[126,2]{0,1:T(2,128)S(1)}, s32[126,2]{0,1:T(2,128)}, u32[]{:S(2)}) %copy-start.9) | copy-done | bytes 1032
  11.3 33.2 %shard_map.100 = f32[16,4096]{1,0:T(8,128)S(1)} custom-call(s32[4,64]{1,0:T(4,128)S(1)} %bitcast.2, s32[2,126]{1,0:T(2,128)S(1)} %bitcast.3, bf16[16,4096]{1,0:T(8,128)(2,1)S(1)} %copy-done.5, s32[1,4096]{1,0:T(1,128)S(1)} %copy-done.6, bf16[64,64,256]{2,1,0:T(8,128)(2,1)S(1)} %copy-done.1, bf16[64,4096]{1,0:T(8,128)(2,1)S(1)} %copy-done.4, ...), custom_call_target="tpu_custom_call" | custom-call | tf_op jit(solution)/shard_map/pallas_call | solution.py:416
  44.5 0.7 %copy.12 = f32[16,4096]{1,0:T(8,128)} copy(f32[16,4096]{1,0:T(8,128)S(1)} %shard_map.100) | data formatting | bytes 524288
Async XLA Ops:
  0.0 2.2 %copy-start = (bf16[256,64,128]{2,1,0:T(8,128)(2,1)S(1)}, bf16[256,64,128]{2,1,0:T(8,128)(2,1)}, u32[]{:S(2)}) copy-start(bf16[256,64,128]{2,1,0:T(8,128)(2,1)} %top_hbm.1) | copy-start | bytes 12582916
  2.2 1.6 %copy-start.1 = (bf16[64,64,256]{2,1,0:T(8,128)(2,1)S(1)}, bf16[64,64,256]{2,1,0:T(8,128)(2,1)}, u32[]{:S(2)}) copy-start(bf16[64,64,256]{2,1,0:T(8,128)(2,1)} %near_hbm.1) | copy-start | bytes 6291460
  3.8 1.6 %copy-start.2 = (bf16[126,64,128]{2,1,0:T(8,128)(2,1)S(1)}, bf16[126,64,128]{2,1,0:T(8,128)(2,1)}, u32[]{:S(2)}) copy-start(bf16[126,64,128]{2,1,0:T(8,128)(2,1)} %coupling_hbm.1) | copy-start | bytes 6193156
  5.4 1.2 %copy-start.3 = (bf16[63,64,128]{2,1,0:T(8,128)(2,1)S(1)}, bf16[63,64,128]{2,1,0:T(8,128)(2,1)}, u32[]{:S(2)}) copy-start(bf16[63,64,128]{2,1,0:T(8,128)(2,1)} %transfer_hbm.1) | copy-start | bytes 3096580
  6.6 1.0 %copy-start.4 = (bf16[64,4096]{1,0:T(8,128)(2,1)S(1)}, bf16[64,4096]{1,0:T(8,128)(2,1)}, u32[]{:S(2)}) copy-start(bf16[64,4096]{1,0:T(8,128)(2,1)} %bases_hbm.1) | copy-start | bytes 1572868
  7.6 0.9 %copy-start.5 = (bf16[16,4096]{1,0:T(8,128)(2,1)S(1)}, bf16[16,4096]{1,0:T(8,128)(2,1)}, u32[]{:S(2)}) copy-start(bf16[16,4096]{1,0:T(8,128)(2,1)} %measured_hbm.1) | copy-start | bytes 393220
  8.5 0.7 %copy-start.6 = (s32[1,4096]{1,0:T(1,128)S(1)}, s32[1,4096]{1,0:T(1,128)}, u32[]{:S(2)}) copy-start(s32[1,4096]{1,0:T(1,128)} %perm_hbm.1) | copy-start | bytes 49156
  9.2 0.7 %copy-start.7 = (bf16[1,4096]{1,0:T(2,128)(2,1)S(1)}, bf16[1,4096]{1,0:T(2,128)(2,1)}, u32[]{:S(2)}) copy-start(bf16[1,4096]{1,0:T(2,128)(2,1)} %root_hbm.1) | copy-start | bytes 24580
  10.0 0.7 %copy-start.8 = (s32[64,4]{0,1:T(4,128)S(1)}, s32[64,4]{0,1:T(4,128)}, u32[]{:S(2)}) copy-start(s32[64,4]{0,1:T(4,128)} %param.12) | copy-start | bytes 3076
  10.6 0.7 %copy-start.9 = (s32[126,2]{0,1:T(2,128)S(1)}, s32[126,2]{0,1:T(2,128)}, u32[]{:S(2)}) copy-start(s32[126,2]{0,1:T(2,128)} %param.16) | copy-start | bytes 3028
